TPU v7x, 256 devices: a whole 4x4x8 slice. The times are simulated.
256 devices in a mesh: dp: 64 (over z, x, core), tensor: 4 (over y).
Axes of the slice: x: 4, y: 4, z: 8, core: 2. Of those that a mesh axis runs over, the one named last changes fastest.
Arguments:
- normed_input: bfloat16 [131072, 896], P(('dp', 'tensor')), may hold values from -6 to 6
- grad_query: bfloat16 [131072, 896], P('dp', 'tensor'), may hold values from -6 to 6
- grad_key: bfloat16 [131072, 128], P('dp', 'tensor'), may hold values from -6 to 6
- grad_value: bfloat16 [131072, 128], P('dp', 'tensor'), may hold values from -6 to 6
- context: bfloat16 [131072, 896], P('dp', 'tensor'), may hold values from -6 to 6
- grad_output: bfloat16 [131072, 896], P(('dp', 'tensor')), may hold values from -6 to 6
- w_query: bfloat16 [896, 896], P(None, 'tensor'), may hold values from -0.1875 to 0.1875
- w_key: bfloat16 [896, 128], P(None, 'tensor'), may hold values from -0.1875 to 0.1875
- w_value: bfloat16 [896, 128], P(None, 'tensor'), may hold values from -0.1875 to 0.1875
- w_output: bfloat16 [896, 896], P('tensor'), may hold values from -0.1875 to 0.1875
- error: float32 [57344, 2048], P('dp', 'tensor'), may hold values from -4 to 4
- factor_init: float32 [2048, 32], P('tensor'), may hold values from -1.5 to 3.5
Outputs:
- grad_input: bfloat16 [131072, 896], P(('dp', 'tensor'))
- grad_context: bfloat16 [131072, 896], P('dp', 'tensor')
- new_error: float32 [57344, 2048], P('dp', 'tensor')
- compressed_grad: float32 [896, 2048], P(None, 'tensor')
All inputs are finite; a program needn't handle non-finite values.
Results may differ from a plain program's by a relative error of at most 0.00045.
Values may be sent and summed in bfloat16 or wider, within the bound.
A program may use at most 128 MiB of HBM per device.

v0:
```python
import jax
import jax.numpy as jnp
from jax import lax
from jax.sharding import PartitionSpec as P

precise = lax.Precision.HIGHEST


def self_gram(left_factor):
    return jnp.einsum("bdr,bds->brs", left_factor, left_factor, precision=precise)


def cholesky_basis(left_factor, gram_matrix):
    lower_factor = jnp.linalg.cholesky(gram_matrix)
    solved = jax.scipy.linalg.solve_triangular(
        lower_factor, jnp.swapaxes(left_factor, 1, 2), lower=True
    )
    return jnp.swapaxes(solved, 1, 2)


def on_device(
    normed_input,
    grad_query,
    grad_key,
    grad_value,
    context,
    grad_output,
    w_query,
    w_key,
    w_value,
    w_output,
    error,
    factor_init,
):
    query_cols = grad_query.shape[1]
    kv_cols = grad_key.shape[1]
    tok_rows = context.shape[0]
    grad_scale = float(tok_rows) ** (-0.5)
    cotangents = jnp.concatenate((grad_query, grad_key, grad_value), 1)
    matched = cotangents
    grad_qkv = jnp.einsum(
        "td,tc->dc",
        lax.all_gather(normed_input, "tensor", axis=0, tiled=True),
        matched,
        preferred_element_type=jnp.float32,
    )
    shard_part = lax.all_gather(grad_output, "tensor", axis=0, tiled=True)
    matched = context
    grad_out_t = jnp.einsum("td,tc->dc", shard_part, matched, preferred_element_type=jnp.float32)
    partial_ctx = jnp.einsum(
        "td,cd->tc", shard_part, w_output, preferred_element_type=jnp.float32
    ).astype(jnp.bfloat16)
    grad_out_t, grad_context = (grad_out_t, partial_ctx)
    grad_input = lax.psum_scatter(
        jnp.einsum("tc,dc->td", grad_query, w_query, preferred_element_type=jnp.float32)
        + jnp.einsum("tc,dc->td", grad_key, w_key, preferred_element_type=jnp.float32)
        + jnp.einsum("tc,dc->td", grad_value, w_value, preferred_element_type=jnp.float32),
        "tensor",
        scatter_dimension=0,
        tiled=True,
    ).astype(jnp.bfloat16)
    merged = jnp.concatenate((grad_qkv, grad_out_t), 1) * grad_scale + error
    edges = (
        (0, query_cols),
        (query_cols, query_cols + 2 * kv_cols),
        (query_cols + 2 * kv_cols, 2 * query_cols + 2 * kv_cols),
    )
    left_terms = jnp.stack(
        [
            jnp.dot(merged[:, lo_col:hi_col], factor_init[lo_col:hi_col], precision=precise)
            for lo_col, hi_col in edges
        ]
    )
    left_factor = lax.psum(left_terms, "dp")
    basis_cols = cholesky_basis(left_factor, self_gram(left_factor))
    right_local = jnp.concatenate(
        [
            jnp.einsum("dc,dr->cr", merged[:, lo_col:hi_col], basis_cols[place], precision=precise)
            for place, (lo_col, hi_col) in enumerate(edges)
        ],
        0,
    )
    right_total = lax.psum(right_local, "dp")
    approx = jnp.concatenate(
        [
            jnp.einsum(
                "dr,cr->dc", basis_cols[place], right_local[lo_col:hi_col], precision=precise
            )
            for place, (lo_col, hi_col) in enumerate(edges)
        ],
        1,
    )
    new_error = merged - approx
    compressed_grad = jnp.concatenate(
        [
            jnp.einsum(
                "dr,cr->dc", basis_cols[place], right_total[lo_col:hi_col], precision=precise
            )
            for place, (lo_col, hi_col) in enumerate(edges)
        ],
        1,
    )
    return (grad_input, grad_context, new_error, compressed_grad)


def solution(mesh):
    return jax.shard_map(
        on_device,
        mesh=mesh,
        in_specs=(
            P(("dp", "tensor"), None),
            P("dp", "tensor"),
            P("dp", "tensor"),
            P("dp", "tensor"),
            P("dp", "tensor"),
            P(("dp", "tensor"), None),
            P(None, "tensor"),
            P(None, "tensor"),
            P(None, "tensor"),
            P("tensor", None),
            P("dp", "tensor"),
            P("tensor", None),
        ),
        out_specs=(
            P(("dp", "tensor"), None),
            P("dp", "tensor"),
            P("dp", "tensor"),
            P(None, "tensor"),
        ),
        check_vma=False,
    )
```

profile of v0, /device:TPU:1, one launch (start us, length us, event | category | flops | bytes accessed | tf_op | source)
XLA Modules:
  0.0 566.7 jit_solution(5376749380798665931)
XLA Ops:
  7.2 0.0 copy-start
  7.2 0.0 all-gather.3.cloned.1.call-start
  7.2 0.7 all-gather.3.cloned.1.call-update
  7.9 0.0 all-gather.5.cloned.1.call-start
  8.0 0.7 all-gather.5.cloned.1.call-update
  8.7 0.0 copy-start.4
  8.7 0.0 copy-start.9
  8.7 0.0 all-reduce.3.cloned.1.call-start
  8.7 2.7 copy.21
  11.5 0.0 copy-done.4
  11.5 0.0 copy-done.9
  11.5 0.0 copy-start.3
  11.5 4.1 fusion.32
  15.6 0.0 copy-done.2
  15.6 0.0 copy-done.3
  15.6 4.3 fusion.31
  19.9 40.3 %all-gather.3.cloned.1.call-done = bf16[2048,896]{1,0:T(8,128)(2,1)} async-done(((bf16[512,896]{1,0:T(8,128)(2,1)}), bf16[2048,896]{1,0:T(8,128)(2,1)}) %all-gather.3.cloned.1.call-update) | async-done | bytes 3670032 | tf_op jit(solution)/shard_map/all_gather | solution.py:47
  60.2 0.0 copy-done
  60.2 3.2 fusion.34
  63.3 45.4 %all-gather.5.cloned.1.call-done = bf16[2048,896]{1,0:T(8,128)(2,1)} async-done(((bf16[512,896]{1,0:T(8,128)(2,1)}), bf16[2048,896]{1,0:T(8,128)(2,1)}) %all-gather.5.cloned.1.call-update) | async-done | bytes 3670032 | tf_op jit(solution)/shard_map/all_gather | solution.py:43
  108.7 0.0 copy-done.5
  108.8 3.5 convolution_bitcast_fusion
  112.3 0.0 copy-done.1
  112.3 0.0 copy-start.7
  112.3 0.2 fusion
  112.5 0.6 copy-done.7
  113.2 0.7 convolution_bitcast_fusion.1
  113.8 0.3 convolution_bitcast_fusion.2
  114.1 0.6 convolution_bitcast_fusion.3
  114.8 0.8 pad_maximum_fusion.1
  115.6 0.0 all-reduce.3.cloned.1.call-update
  115.6 0.0 all-reduce.5.cloned.1.call-start
  115.7 177.8 %all-reduce.3.cloned.1.call-done = f32[3,896,32]{1,2,0:T(8,128)} async-done(((f32[3,896,32]{1,2,0:T(8,128)}), f32[3,896,32]{1,2,0:T(8,128)}) %all-reduce.3.cloned.1.call-update) | async-done | bytes 344080 | tf_op jit(solution)/shard_map/psum | solution.py:74
  293.4 1.5 fusion.33
  295.0 0.0 copy-start.6
  295.0 0.0 copy-start.8
  295.0 0.1 copy.22
  295.1 8.8 %custom-call.8 = f32[3,32,32]{2,1,0:T(8,128)S(1)} custom-call(f32[3,32,32]{2,1,0:T(8,128)S(1)} %fusion.23), custom_call_target="Cholesky" | custom-call | tf_op jit(solution)/shard_map/jit(cholesky)/cholesky | solution.py:14
  304.0 0.1 compare_reduce_fusion
  304.1 0.1 select_bitcast_fusion
  304.2 7.4 %custom-call.9 = f32[3,1,32,32]{2,3,1,0:T(8,128)S(1)} custom-call(f32[3,1,32,32]{3,2,1,0:T(8,128)S(1)} %select_bitcast_fusion), custom_call_target="InvertDiagBlocksLowerTriangular" | custom-call | tf_op jit(solution)/shard_map/jit(_solve_triangular)/vmap()/triangular_solve | solution.py:15
  311.5 1.5 fusion.21
  313.0 0.9 fusion.6
  313.9 0.3 fusion.12
  314.3 0.9 fusion.9
  315.2 0.7 pad_maximum_fusion.2
  315.9 0.0 all-reduce.5.cloned.1.call-update
  315.9 0.2 reduce-scatter.2.cloned.1.call-start
  316.2 9.3 %add_add_fusion = f32[2048,896]{1,0:T(8,128)} fusion(f32[2048,896]{1,0:T(8,128)} %fusion.31, f32[2048,896]{1,0:T(8,128)} %fusion.32, bf16[2048,32]{0,1:T(8,128)(2,1)S(1)} %copy-done.6, bf16[896,32]{0,1:T(8,128)(2,1)S(1)} %copy-done.8), kind=kOutput, calls=%fused_computation | convolution fusion | flops 121110528 | bytes 22208512 | tf_op jit(solution)/shard_map/tc,dc->td/dot_general | solution.py:57
  325.5 0.0 reduce-scatter.2.cloned.1.call-update
  325.5 4.4 convolution_convert_fusion
  329.9 0.4 fusion.18
  330.3 0.8 fusion.20
  331.1 0.8 fusion.16
  332.0 1.5 maximum_subtract_fusion
  333.5 2.7 copy.24
  336.2 146.8 %all-reduce.5.cloned.1.call-done = f32[512,32]{0,1:T(8,128)} async-done(((f32[512,32]{0,1:T(8,128)}), f32[512,32]{0,1:T(8,128)}) %all-reduce.5.cloned.1.call-update) | async-done | bytes 65552 | tf_op jit(solution)/shard_map/psum | solution.py:83
  483.0 1.2 fusion.17
  484.2 1.7 fusion.19
  485.9 1.6 fusion.15
  487.5 0.1 pad_maximum_fusion
  487.6 1.7 copy.25
  489.3 68.3 %reduce-scatter.2.cloned.1.call-done = f32[512,896]{1,0:T(8,128)} async-done(((f32[2048,896]{1,0:T(8,128)}), f32[512,896]{1,0:T(8,128)}) %reduce-scatter.2.cloned.1.call-update) | async-done | bytes 1835024 | tf_op jit(solution)/shard_map/reduce_scatter | solution.py:54
  557.6 2.5 convert_element_type.6
  (9 shorter events, 0.1 us)
Async XLA Ops:
  7.2 53.0 %copy-start = (bf16[2048,224]{0,1:T(8,128)(2,1)S(1)}, bf16[2048,224]{0,1:T(8,128)(2,1)}, u32[]{:S(2)}) copy-start(bf16[2048,224]{0,1:T(8,128)(2,1)} %param.16) | copy-start | bytes 2752516
  7.2 53.0 %all-gather.3.cloned.1.call-start = ((), (), s32[]{:S(2)}) async-start(), calls=%async_computation.2 | async-start | bytes 4587520 | tf_op jit(solution)/shard_map/all_gather | solution.py:47
  7.9 100.8 %all-gather.5.cloned.1.call-start = ((), (), s32[]{:S(2)}) async-start(), calls=%async_computation.3 | async-start | bytes 4587520 | tf_op jit(solution)/shard_map/all_gather | solution.py:43
  8.7 2.8 copy-start.4
  8.7 2.8 copy-start.9
  8.7 284.8 %all-reduce.3.cloned.1.call-start = ((), (), s32[]{:S(2)}) async-start(), calls=%async_computation.4 | async-start | bytes 688128 | tf_op jit(solution)/shard_map/psum | solution.py:74
  11.5 4.1 copy-start.2
  11.5 4.1 copy-start.3
  19.9 88.9 %copy-start.5 = (bf16[2048,32]{0,1:T(8,128)(2,1)S(1)}, bf16[2048,32]{0,1:T(8,128)(2,1)}, u32[]{:S(2)}) copy-start(bf16[2048,32]{0,1:T(8,128)(2,1)} %param.15) | copy-start | bytes 393220
  108.8 3.6 copy-start.1
  112.3 0.8 copy-start.7
  115.6 367.4 %all-reduce.5.cloned.1.call-start = ((), (), s32[]{:S(2)}) async-start(), calls=%async_computation.5 | async-start | bytes 131072 | tf_op jit(solution)/shard_map/psum | solution.py:83
  295.0 21.1 %copy-start.6 = (bf16[2048,32]{0,1:T(8,128)(2,1)S(1)}, bf16[2048,32]{0,1:T(8,128)(2,1)}, u32[]{:S(2)}) copy-start(bf16[2048,32]{0,1:T(8,128)(2,1)} %param.15) | copy-start | bytes 393220
  295.0 21.1 %copy-start.8 = (bf16[896,32]{0,1:T(8,128)(2,1)S(1)}, bf16[896,32]{0,1:T(8,128)(2,1)}, u32[]{:S(2)}) copy-start(bf16[896,32]{0,1:T(8,128)(2,1)} %param.20) | copy-start | bytes 172036
  315.9 241.7 %reduce-scatter.2.cloned.1.call-start = ((), (), s32[]{:S(2)}) async-start(), calls=%async_computation.1 | async-start | bytes 9175040 | tf_op jit(solution)/shard_map/reduce_scatter | solution.py:54
Sparse Core Ops, SparseCore 0:
  9.8 50.2 all-gather.2
  62.0 46.7 all-gather.4
  115.7 177.7 all-reduce.2
  316.0 166.8 all-reduce.4
  485.5 72.0 reduce-scatter.1
where the time goes:
time: 567 us
  waiting for transfers between devices  480 us (85%)
  matrix products  42.1 us (7%)
  other arithmetic  22.2 us (4%)
  between operations  14 us (2%)
  local copies, waits for them, and re-layouts  7.89 us (1%)
    psum x1, waiting for transfers between devices, on_device(): left_factor = lax.psum(left_terms, 'dp')  178 us
    psum x1, waiting for transfers between devices, on_device(): right_total = lax.psum(right_local, 'dp')  147 us
    reduce_scatter x1, waiting for transfers between devices, on_device(): lax.psum_scatter(jnp.einsum('tc,dc->td', grad_query, w_query, preferred_e...  68.3 us
    all_gather x1, waiting for transfers between devices, on_device(): lax.all_gather(normed_input, 'tensor', axis=0, tiled=True)  45.4 us
    all_gather x1, waiting for transfers between devices, on_device(): shard_part = lax.all_gather(grad_output, 'tensor', axis=0, tiled=True)  40.3 us
  transfers between devices with their start and end apart: 5, of which 5 were waited for; matrix products, arithmetic and copies ran while one was open for 7% of the time, Pallas kernels for 0%

commit v1 on v0

v1 whole, which is shorter than its diff:
```python
import jax
import jax.numpy as jnp
from jax import lax
from jax.experimental import pallas as pl
from jax.experimental.pallas import tpu as pltpu
from jax.sharding import PartitionSpec as P

MESH = pl.DeviceIdType.MESH
F32, BF16 = jnp.float32, jnp.bfloat16
PRECISE = lax.Precision.HIGHEST
NZ, NX, NC, NY = 8, 4, 2, 4
D = 896
TOK = 2048
ROWS = TOK // NY
HALF = ROWS // 2
QC, KC = 224, 32
PACK = 512
XC = QC + 2 * KC
WL = 1024
WX = WL // 4
RANK = 32
NB = 3
NR = NB * RANK
PIECES = NC * NX
PR = NR // PIECES
WR = XC // NC


def nt(a, b, precision=None):
    return lax.dot_general(
        a, b, (((1,), (1,)), ((), ())), precision=precision, preferred_element_type=F32
    )


def tn(a, b, precision=None):
    return lax.dot_general(
        a, b, (((0,), (0,)), ((), ())), precision=precision, preferred_element_type=F32
    )


def nn(a, b, precision=None):
    return jnp.dot(a, b, precision=precision, preferred_element_type=F32)


def split3(a):
    hi = a.astype(BF16)
    rest = a - hi.astype(F32)
    mid = rest.astype(BF16)
    low = (rest - mid.astype(F32)).astype(BF16)
    return hi, mid, low


def in_block(shape):
    row = lax.broadcasted_iota(jnp.int32, shape, 0)
    col = lax.broadcasted_iota(jnp.int32, shape, 1)
    block = (col >= QC).astype(jnp.int32) + (col >= XC).astype(jnp.int32)
    return (row // RANK) == block


def rcopy(src, dst, send, recv, dev):
    return pltpu.make_async_remote_copy(
        src_ref=src, dst_ref=dst, send_sem=send, recv_sem=recv, device_id=dev, device_id_type=MESH
    )


def inverse_factor(gram):
    row = lax.broadcasted_iota(jnp.int32, (RANK, RANK), 0)
    col = lax.broadcasted_iota(jnp.int32, (RANK, RANK), 1)
    eye = (row == col).astype(F32)
    work = jnp.concatenate([eye, gram], axis=1)
    sub = lax.broadcasted_iota(jnp.int32, (RANK, 2 * RANK), 0)
    for k in range(RANK):
        pivot = work[k : k + 1, RANK + k : RANK + k + 1]
        inv = 1.0 / jnp.sqrt(pivot)
        row_k = work[k : k + 1, :] * inv
        col_k = work[:, RANK + k : RANK + k + 1] * inv
        work = jnp.where(sub > k, work - col_k * row_k, jnp.where(sub == k, row_k, work))
    return work[:, :RANK]


def body(
    X, DQ, DK, DV, CX, DO, WQ, WK, WV, WO, ER, FI,
    GI, GC, NE, CG,
    xg, og, cot, wo, er, fi, wf, qf, acc,
    pts, ptr, lts, rcore, s1, rx, sz, rz, sy, ry, gl, lt, bas,
    rt, rcr, q1, rxr, q2, rzr, gr, rtot,
    giv, gcv, nev, cgv,
    ld, st, ag_s, ag_r, fw_s, fw_r, p_s, p_r, c_s, c_r, x_s, x_r, z_s, z_r, w_s, w_r, y_s, y_r, q_s, q_r,
):
    d = lax.axis_index("dp")
    y = lax.axis_index("tensor")
    z, x, c = d // (NX * NC), (d // NC) % NX, d % NC

    def dev(z_, x_, c_, y_):
        return ((z_ * NX + x_) * NC + c_, y_)

    core_dev = dev(z, x, 1 - c, y)
    x_dev = [dev(z, (x + k) % NX, c, y) for k in range(NX)]
    z_dev = [dev((z + k) % NZ, x, c, y) for k in range(NZ)]
    y_dev = [dev(z, x, c, (y + k) % NY) for k in range(NY)]

    def start(copies):
        for cp in copies:
            cp.start()

    def wait(copies):
        for cp in copies:
            cp.wait()

    barrier = pltpu.get_barrier_semaphore()
    peers = [core_dev] + x_dev[1:] + z_dev[1:] + y_dev[1:]
    for p in peers:
        pl.semaphore_signal(barrier, inc=1, device_id=p, device_id_type=MESH)

    pairs = [
        (WQ, wf.at[0, 0:QC, 0:D]), (WK, wf.at[0, QC : QC + KC, 0:D]), (WV, wf.at[0, QC + KC : XC, 0:D]),
        (DQ, cot.at[0:QC]), (DK, cot.at[QC : QC + KC]), (DV, cot.at[QC + KC : XC]), (CX, cot.at[XC:PACK]),
        (FI, fi), (ER, er), (X, xg.at[0]), (DO, og.at[0]), (WO, wo),
    ]
    loads = [pltpu.make_async_copy(a, b, ld.at[i]) for i, (a, b) in enumerate(pairs)]
    start(loads)
    wf[0, :, D:] = jnp.zeros((XC, WL - D), BF16)
    wait(loads[:3])
    pl.semaphore_wait(barrier, len(peers))

    wrows, wcols = pl.ds(pl.multiple_of(c * WR, 16), WR), pl.ds(pl.multiple_of(x * WX, 128), WX)
    w_y = [rcopy(wf.at[0, wrows, wcols], wf.at[k, wrows, wcols], y_s.at[1, k], y_r.at[1, k], y_dev[NY - k])
           for k in range(1, NY)]
    start(w_y)

    wait(loads[3:8])
    fm = jnp.where(in_block((NR, PACK)), jnp.concatenate([fi[...]] * NB, axis=0), 0.0)
    fm3 = jnp.concatenate(split3(fm), axis=0)

    def token_cols(k):
        return pl.ds(pl.multiple_of(((y + NY - k) % NY) * ROWS, ROWS), ROWS)

    for k in (1, 3, 2, 0):
        prod = nn(fm3, cot[:, token_cols(k)])
        dst = ptr if k == 0 else pts
        dst[k] = prod[:NR] + prod[NR : 2 * NR] + prod[2 * NR :]
    p_y = [rcopy(pts.at[k], ptr.at[k], p_s.at[k], p_r.at[k], y_dev[NY - k]) for k in (1, 3, 2)]
    start(p_y)

    def own_sends(i, src, dst):
        out = []
        for n in range(2):
            for way in (1, 3):
                h = n if way == 1 else 1 - n
                rows = pl.ds(h * HALF, HALF)
                out.append(rcopy(src.at[rows], dst.at[way, rows],
                                 ag_s.at[i, way, h], ag_r.at[i, way, h], y_dev[way]))
        return out

    def forwards(i, buf):
        out = []
        for h, way in ((0, 1), (1, 3)):
            rows = pl.ds(h * HALF, HALF)
            out.append(rcopy(buf.at[way, rows], buf.at[2, rows], fw_s.at[i, h], fw_r.at[i, h], y_dev[way]))
        return out

    own_o, own_x = own_sends(0, DO, og), own_sends(1, X, xg)
    fwd_o, fwd_x = forwards(0, og), forwards(1, xg)
    start(own_o)
    start(own_x)

    wait(w_y)
    w_x = [rcopy(wf.at[pl.ds(1, NY - 1), wrows, wcols], wf.at[pl.ds(1, NY - 1), wrows, wcols],
                 w_s.at[k], w_r.at[k], x_dev[k]) for k in range(1, NX)]
    start(w_x)

    def grads_x(slot):
        acc[0:XC, :] += nn(cot[0:XC, token_cols(slot)], xg[slot])

    def grads_o(slot):
        acc[XC:PACK, :] += nn(cot[XC:PACK, token_cols(slot)], og[slot])

    def contexts(slot):
        gcv[:, token_cols(slot)] = nt(wo[...], og[slot]).astype(BF16)

    scale = float(TOK) ** (-0.5)
    wait(loads[8:])
    own_e = nt(fm, er[...], PRECISE)
    acc[...] = er[...].T * (float(TOK) ** 0.5)
    grads_x(0)
    grads_o(0)
    contexts(0)

    wait(p_y)
    for k in range(NY):
        parts = split3(ptr[k])
        up = nn(jnp.concatenate([t[: 2 * RANK] for t in parts], axis=0), xg[0])
        lo = nn(jnp.concatenate([t[2 * RANK :] for t in parts], axis=0), og[0])
        up = up[: 2 * RANK] + up[2 * RANK : 4 * RANK] + up[4 * RANK :]
        lo = lo[:RANK] + lo[RANK : 2 * RANK] + lo[2 * RANK :]
        left = jnp.concatenate([up, lo], axis=0) * scale
        if k == 0:
            left = left + own_e
        for p in range(PIECES):
            lts[p, k * PR : (k + 1) * PR, :] = left[p * PR : (p + 1) * PR, :]

    lc = rcopy(lts.at[pl.ds(NX * (1 - c), NX)], rcore, c_s.at[0], c_r.at[0], core_dev)
    lc.start()
    wait(w_x)
    w_c = rcopy(wf.at[pl.ds(1, NY - 1), wrows], wf.at[pl.ds(1, NY - 1), wrows], c_s.at[4], c_r.at[4], core_dev)
    lc.wait()
    w_c.start()
    s1[...] = lts[pl.ds(NX * c, NX)] + rcore[...]
    lx = [rcopy(s1.at[(x + k) % NX], rx.at[k], x_s.at[0, k], x_r.at[0, k], x_dev[k]) for k in range(1, NX)]
    start(lx)
    wait(lx)
    s2 = s1[x] + rx[1] + rx[2] + rx[3]
    for i in range(NZ - 1):
        sz[i] = s2[:, i * 128 : (i + 1) * 128]
    sz[NZ - 1] = jnp.zeros_like(sz[NZ - 1])
    lz = [rcopy(sz.at[(z + k) % NZ], rz.at[k], z_s.at[0, k], z_r.at[0, k], z_dev[k]) for k in range(1, NZ)]
    start(lz)
    wait(lz)
    s3 = sz[z]
    for k in range(1, NZ):
        s3 = s3 + rz[k]
    sy[...] = jnp.zeros_like(sy)
    for k in range(NY):
        sy[k, 0:PR, :] = s3[k * PR : (k + 1) * PR, :]
    ly = [rcopy(sy.at[k], ry.at[k], y_s.at[0, k], y_r.at[0, k], y_dev[k]) for k in range(1, NY)]
    start(ly)
    wait(own_o)
    start(fwd_o)
    for slot in (1, 3):
        grads_o(slot)
        contexts(slot)
    wait(ly)
    gl[c, x, z] = sy[0] + ry[1] + ry[2] + ry[3]
    gz = [rcopy(gl.at[c, x, z], gl.at[c, x, z], z_s.at[1, k], z_r.at[1, k], z_dev[k]) for k in range(1, NZ)]
    start(gz)
    wait(own_x)
    start(fwd_x)
    q_y = [rcopy(cot.at[0:XC, token_cols(k)], qf.at[k], q_s.at[k], q_r.at[k], y_dev[NY - k]) for k in (1, 3, 2)]
    start(q_y)
    wait(gz)
    gx = [rcopy(gl.at[c, x], gl.at[c, x], x_s.at[1, k], x_r.at[1, k], x_dev[k]) for k in range(1, NX)]
    start(gx)
    grads_x(1)
    wait(gx)
    gc = rcopy(gl.at[c], gl.at[c], c_s.at[1], c_r.at[1], core_dev)
    gc.start()
    grads_x(3)
    gc.wait()
    for p in range(PIECES):
        for i in range(NZ - 1):
            lt[p * PR : (p + 1) * PR, i * 128 : (i + 1) * 128] = gl[p // NX, p % NX, i, 0:PR, :]
    for b in range(NB):
        left = lt[b * RANK : (b + 1) * RANK, :]
        bas[b * RANK : (b + 1) * RANK, :] = nn(inverse_factor(nt(left, left, PRECISE)), left, PRECISE)

    wait(fwd_o)
    grads_o(2)
    contexts(2)
    out_gc = pltpu.make_async_copy(gcv, GC, st.at[1])
    out_gc.start()
    wait(fwd_x)
    grads_x(2)
    acc[...] = acc[...] * scale

    right = jnp.where(in_block((NR, PACK)), nt(bas[...], acc[...], PRECISE), 0.0)
    rt[...] = right[:RANK] + right[RANK : 2 * RANK] + right[2 * RANK :]
    hr = RANK // NC
    rc = rcopy(rt.at[pl.ds(pl.multiple_of((1 - c) * hr, 8), hr)], rcr, c_s.at[2], c_r.at[2], core_dev)
    rc.start()
    rc.wait()
    s = rt[pl.ds(pl.multiple_of(c * hr, 8), hr), :] + rcr[...]
    for i in range(NX):
        q1[i] = s[:, i * 128 : (i + 1) * 128]
    rxs = [rcopy(q1.at[(x + k) % NX], rxr.at[k], x_s.at[2, k], x_r.at[2, k], x_dev[k]) for k in range(1, NX)]
    start(rxs)
    wait(rxs)
    q2[...] = q1[x] + rxr[1] + rxr[2] + rxr[3]
    rzs = [rcopy(q2, rzr.at[k], z_s.at[2, k], z_r.at[2, k], z_dev[k]) for k in range(1, NZ)]
    start(rzs)
    nev[...] = acc[...].T - tn(bas[...], right, PRECISE)
    out_ne = pltpu.make_async_copy(nev, NE, st.at[2])
    out_ne.start()
    wait(rzs)
    rzr[0] = q2[...]
    total = rzr[z % NZ]
    for i in range(1, NZ):
        total = total + rzr[(z + NZ - i) % NZ]
    gr[c, x] = total
    rxg = [rcopy(gr.at[c, x], gr.at[c, x], x_s.at[3, k], x_r.at[3, k], x_dev[k]) for k in range(1, NX)]
    start(rxg)
    wait(rxg)
    rcg = rcopy(gr.at[c], gr.at[c], c_s.at[3], c_r.at[3], core_dev)
    rcg.start()
    rcg.wait()
    for p in range(NC):
        for i in range(NX):
            rtot[p * hr : (p + 1) * hr, i * 128 : (i + 1) * 128] = gr[p, i]
    full = jnp.where(in_block((NR, PACK)), jnp.concatenate([rtot[...]] * NB, axis=0), 0.0)
    cgv[...] = tn(bas[...], full, PRECISE)
    out_cg = pltpu.make_async_copy(cgv, CG, st.at[3])
    out_cg.start()

    w_c.wait()
    wait(q_y)
    out = tn(cot[0:XC, token_cols(0)], wf[0, :, 0:D])
    for k in range(1, NY):
        out = out + tn(qf[k], wf[k, :, 0:D])
    giv[...] = out.astype(BF16)
    out_gi = pltpu.make_async_copy(giv, GI, st.at[0])
    out_gi.start()
    wait((out_gc, out_ne, out_cg, out_gi))


def on_device(
    normed_input, grad_query, grad_key, grad_value, context, grad_output,
    w_query, w_key, w_value, w_output, error, factor_init,
):
    any_spec = pl.BlockSpec(memory_space=pl.ANY)
    V = pltpu.VMEM
    hr = RANK // NC
    scratch = [
        V((NY, ROWS, D), BF16), V((NY, ROWS, D), BF16), V((PACK, TOK), BF16),
        V((QC, D), BF16), V((D, PACK), F32), V((RANK, PACK), F32),
        V((NY, XC, WL), BF16), V((NY, XC, ROWS), BF16), V((PACK, D), F32),
        V((NY, NR, ROWS), F32), V((NY, NR, ROWS), F32),
        V((PIECES, NY * PR, D), F32), V((NX, NY * PR, D), F32), V((NX, NY * PR, D), F32),
        V((NX, NY * PR, D), F32), V((NZ, NY * PR, 128), F32), V((NZ, NY * PR, 128), F32),
        V((NY, 16, 128), F32), V((NY, 16, 128), F32), V((NC, NX, NZ, 16, 128), F32),
        V((NR, D), F32), V((NR, D), F32),
        V((RANK, PACK), F32), V((hr, PACK), F32), V((NX, hr, 128), F32), V((NX, hr, 128), F32),
        V((hr, 128), F32), V((NZ, hr, 128), F32), V((NC, NX, hr, 128), F32), V((RANK, PACK), F32),
        V((ROWS, D), BF16), V((QC, TOK), BF16), V((D, PACK), F32), V((D, PACK), F32),
    ]
    S = pltpu.SemaphoreType.DMA
    sems = [
        S((12,)), S((4,)), S((2, 4, 2)), S((2, 4, 2)), S((2, 2)), S((2, 2)), S((NY,)), S((NY,)),
        S((5,)), S((5,)), S((4, NX)), S((4, NX)), S((3, NZ)), S((3, NZ)),
        S((NX,)), S((NX,)), S((2, NY)), S((2, NY)), S((NY,)), S((NY,)),
    ]
    grad_input, grad_context, new_error, compressed = pl.pallas_call(
        body,
        out_shape=(
            jax.ShapeDtypeStruct((ROWS, D), BF16),
            jax.ShapeDtypeStruct((QC, TOK), BF16),
            jax.ShapeDtypeStruct((D, PACK), F32),
            jax.ShapeDtypeStruct((D, PACK), F32),
        ),
        in_specs=[any_spec] * 12,
        out_specs=(any_spec,) * 4,
        scratch_shapes=scratch + sems,
        compiler_params=pltpu.CompilerParams(
            collective_id=0, has_side_effects=True, vmem_limit_bytes=60 * 2**20
        ),
        name="backward",
    )(
        normed_input, grad_query.T, grad_key.T, grad_value.T, context.T, grad_output,
        w_query.T, w_key.T, w_value.T, w_output, error, factor_init.T,
    )
    return grad_input, grad_context.T, new_error, compressed


def solution(mesh):
    return jax.shard_map(
        on_device,
        mesh=mesh,
        in_specs=(
            P(("dp", "tensor"), None),
            P("dp", "tensor"),
            P("dp", "tensor"),
            P("dp", "tensor"),
            P("dp", "tensor"),
            P(("dp", "tensor"), None),
            P(None, "tensor"),
            P(None, "tensor"),
            P(None, "tensor"),
            P("tensor", None),
            P("dp", "tensor"),
            P("tensor", None),
        ),
        out_specs=(
            P(("dp", "tensor"), None),
            P("dp", "tensor"),
            P("dp", "tensor"),
            P(None, "tensor"),
        ),
        check_vma=False,
    )
```

time: 567 us -> 120 us (0.21)
  waiting for transfers between devices: 480 us -> 0 us
  Pallas kernels: 0 us -> 113 us
  matrix products: 42.1 us -> 0 us
  other arithmetic: 22.2 us -> 0 us
  between operations: 14 us -> 0.66 us
    psum x2 -> x0, waiting for transfers between devices: 325 us -> none  [the longest x1 178 us: on_device(): left_factor = lax.psum(left_terms, 'dp')]
    pallas_call x0 -> x1, Pallas kernels: none -> 113 us  [on_device(): pl.pallas_call(body, out_shape=(jax.ShapeDtypeStruct((ROWS, D), BF16), ja...]
    all_gather x2 -> x0, waiting for transfers between devices: 85.7 us -> none  [the longest x1 45.4 us: on_device(): lax.all_gather(normed_input, 'tensor', axis=0, tiled=True)]
    reduce_scatter x1 -> x0, waiting for transfers between devices: 68.3 us -> none  [on_device(): lax.psum_scatter(jnp.einsum('tc,dc->td', grad_query, w_query, preferred_e...]
    dot_general x19 -> x0, matrix products: 40.6 us -> none  [the longest x1 9.34 us: on_device(): jnp.einsum('tc,dc->td', grad_value, w_value, preferred_element_type=jnp.f...]
    another operation x8 -> x0, other arithmetic: 17.2 us -> none  [the longest x4 8.96 us: cholesky_basis(): lower_factor = jnp.linalg.cholesky(gram_matrix)]
  transfers between devices with their start and end apart: 5 -> 0, of which waited for: 5 -> 0; matrix products, arithmetic and copies ran while one was open for 7% -> 0% of each run, Pallas kernels for 0% -> 0%
where the time goes in v1:
time: 120 us
  Pallas kernels  113 us (94%)
  local copies, waits for them, and re-layouts  6.65 us (6%)
    pallas_call x1, Pallas kernels, on_device(): pl.pallas_call(body, out_shape=(jax.ShapeDtypeStruct((ROWS, D), BF16), ja...  113 us
    unnamed x10, local copies, waits for them, and re-layouts  6.65 us

profile of v1, /device:TPU:1, one launch (start us, length us, event | category | flops | bytes accessed | tf_op | source)
XLA Modules:
  0.0 120.0 jit_solution(6593388258359857990)
XLA Ops:
  0.6 112.7 %backward.1 = (bf16[512,896]{1,0:T(8,128)(2,1)}, bf16[224,2048]{1,0:T(8,128)(2,1)}, f32[896,512]{1,0:T(8,128)}, f32[896,512]{1,0:T(8,128)}) custom-call(bf16[512,896]{1,0:T(8,128)(2,1)} %X.1, bf16[224,2048]{1,0:T(8,128)(2,1)} %bitcast.9, bf16[32,2048]{1,0:T(8,128)(2,1)} %bitcast.13, bf16[32,2048]{1,0:T(8,128)(2,1)} %bitcast.14, bf16[224,2048]{1,0:T(8,128)(2,1)} %bitcast.10, ...), custom_call_target="tpu_custom_call" | custom-call | tf_op jit(solution)/shard_map/backward/pallas_call | solution.py:340
  113.4 0.0 copy-start.2
  113.4 0.0 copy-start.1
  113.4 2.3 %copy.20 = bf16[512,896]{1,0:T(8,128)(2,1)} copy(bf16[512,896]{1,0:T(8,128)(2,1)} %get-tuple-element.16) | data formatting | bytes 1835008
  115.7 0.0 copy-done.2
  115.7 0.9 copy.21
  116.7 0.0 copy-done.1
  116.7 0.0 copy-start
  116.7 1.2 %copy.22 = f32[896,512]{1,0:T(8,128)} copy(f32[896,512]{1,0:T(8,128)S(1)} %copy-done.1) | data formatting | bytes 3670016
  117.9 0.9 copy-done
  118.8 1.2 %copy.23 = f32[896,512]{1,0:T(8,128)} copy(f32[896,512]{1,0:T(8,128)S(1)} %copy-done) | data formatting | bytes 3670016
Async XLA Ops:
  113.4 2.3 %copy-start.2 = (bf16[224,2048]{1,0:T(8,128)(2,1)S(1)}, bf16[224,2048]{1,0:T(8,128)(2,1)}, u32[]{:S(2)}) copy-start(bf16[224,2048]{1,0:T(8,128)(2,1)} %get-tuple-element.9) | copy-start | bytes 2752516
  113.4 3.3 %copy-start.1 = (f32[896,512]{1,0:T(8,128)S(1)}, f32[896,512]{1,0:T(8,128)}, u32[]{:S(2)}) copy-start(f32[896,512]{1,0:T(8,128)} %get-tuple-element.18) | copy-start | bytes 5505028
  116.7 2.2 %copy-start = (f32[896,512]{1,0:T(8,128)S(1)}, f32[896,512]{1,0:T(8,128)}, u32[]{:S(2)}) copy-start(f32[896,512]{1,0:T(8,128)} %get-tuple-element.19) | copy-start | bytes 5505028

commit v2 on v1

--- a/solution.py
+++ b/solution.py
@@ -12,7 +12,8 @@
 D = 896
 TOK = 2048
 ROWS = TOK // NY
-HALF = ROWS // 2
+CH = 4
+CHR = ROWS // CH
 QC, KC = 224, 32
 PACK = 512
 XC = QC + 2 * KC
@@ -80,12 +81,12 @@
 
 def body(
     X, DQ, DK, DV, CX, DO, WQ, WK, WV, WO, ER, FI,
-    GI, GC, NE, CG,
+    GI, GC, NE, BA, GR,
     xg, og, cot, wo, er, fi, wf, qf, acc,
     pts, ptr, lts, rcore, s1, rx, sz, rz, sy, ry, gl, lt, bas,
-    rt, rcr, q1, rxr, q2, rzr, gr, rtot,
-    giv, gcv, nev, cgv,
-    ld, st, ag_s, ag_r, fw_s, fw_r, p_s, p_r, c_s, c_r, x_s, x_r, z_s, z_r, w_s, w_r, y_s, y_r, q_s, q_r,
+    rpart, q1, rxr, q2, rzr, gr,
+    giv, gcv, nev, bav,
+    ld, st, ag_s, ag_r, fw_s, fw_r, p_s, p_r, c_s, c_r, x_s, x_r, z_s, z_r, w_s, w_r, y_s, y_r, q_s, q_r, r_s, r_r,
 ):
     d = lax.axis_index("dp")
     y = lax.axis_index("tensor")
@@ -98,6 +99,8 @@
     x_dev = [dev(z, (x + k) % NX, c, y) for k in range(NX)]
     z_dev = [dev((z + k) % NZ, x, c, y) for k in range(NZ)]
     y_dev = [dev(z, x, c, (y + k) % NY) for k in range(NY)]
+    row = [(e, k) for k in range(NX) for e in range(NC)][1:]
+    row_dev = {(e, k): dev(z, (x + k) % NX, (c + e) % NC, y) for e, k in row}
 
     def start(copies):
         for cp in copies:
@@ -108,7 +111,7 @@
             cp.wait()
 
     barrier = pltpu.get_barrier_semaphore()
-    peers = [core_dev] + x_dev[1:] + z_dev[1:] + y_dev[1:]
+    peers = list(row_dev.values()) + z_dev[1:] + y_dev[1:]
     for p in peers:
         pl.semaphore_signal(barrier, inc=1, device_id=p, device_id_type=MESH)
 
@@ -120,12 +123,33 @@
     loads = [pltpu.make_async_copy(a, b, ld.at[i]) for i, (a, b) in enumerate(pairs)]
     start(loads)
     wf[0, :, D:] = jnp.zeros((XC, WL - D), BF16)
-    wait(loads[:3])
     pl.semaphore_wait(barrier, len(peers))
+
+    def own_sends(i, src, dst):
+        out = []
+        for n in range(CH):
+            for way, h in ((1, n), (3, CH - 1 - n)):
+                rows = pl.ds(h * CHR, CHR)
+                out.append(rcopy(src.at[rows], dst.at[way, rows],
+                                 ag_s.at[i, way, h], ag_r.at[i, way, h], y_dev[way]))
+        return out
+
+    def forwards(i, buf):
+        out = []
+        for n in range(CH // 2):
+            for way, h in ((1, n), (3, CH - 1 - n)):
+                rows = pl.ds(h * CHR, CHR)
+                out.append(rcopy(buf.at[way, rows], buf.at[2, rows], fw_s.at[i, h], fw_r.at[i, h], y_dev[way]))
+        return out
+
+    own_o, own_x = own_sends(0, DO, og), own_sends(1, X, xg)
+    fwd_o, fwd_x = forwards(0, og), forwards(1, xg)
+    start(own_o[:2])
 
     wrows, wcols = pl.ds(pl.multiple_of(c * WR, 16), WR), pl.ds(pl.multiple_of(x * WX, 128), WX)
     w_y = [rcopy(wf.at[0, wrows, wcols], wf.at[k, wrows, wcols], y_s.at[1, k], y_r.at[1, k], y_dev[NY - k])
            for k in range(1, NY)]
+    wait(loads[:3])
     start(w_y)
 
     wait(loads[3:8])
@@ -142,27 +166,8 @@
     p_y = [rcopy(pts.at[k], ptr.at[k], p_s.at[k], p_r.at[k], y_dev[NY - k]) for k in (1, 3, 2)]
     start(p_y)
 
-    def own_sends(i, src, dst):
-        out = []
-        for n in range(2):
-            for way in (1, 3):
-                h = n if way == 1 else 1 - n
-                rows = pl.ds(h * HALF, HALF)
-                out.append(rcopy(src.at[rows], dst.at[way, rows],
-                                 ag_s.at[i, way, h], ag_r.at[i, way, h], y_dev[way]))
-        return out
-
-    def forwards(i, buf):
-        out = []
-        for h, way in ((0, 1), (1, 3)):
-            rows = pl.ds(h * HALF, HALF)
-            out.append(rcopy(buf.at[way, rows], buf.at[2, rows], fw_s.at[i, h], fw_r.at[i, h], y_dev[way]))
-        return out
-
-    own_o, own_x = own_sends(0, DO, og), own_sends(1, X, xg)
-    fwd_o, fwd_x = forwards(0, og), forwards(1, xg)
-    start(own_o)
-    start(own_x)
+    start(own_o[2:])
+    start(own_x[:2])
 
     wait(w_y)
     w_x = [rcopy(wf.at[pl.ds(1, NY - 1), wrows, wcols], wf.at[pl.ds(1, NY - 1), wrows, wcols],
@@ -186,8 +191,7 @@
     grads_o(0)
     contexts(0)
 
-    wait(p_y)
-    for k in range(NY):
+    def left_from(k):
         parts = split3(ptr[k])
         up = nn(jnp.concatenate([t[: 2 * RANK] for t in parts], axis=0), xg[0])
         lo = nn(jnp.concatenate([t[2 * RANK :] for t in parts], axis=0), og[0])
@@ -199,6 +203,11 @@
         for p in range(PIECES):
             lts[p, k * PR : (k + 1) * PR, :] = left[p * PR : (p + 1) * PR, :]
 
+    left_from(0)
+    for cp, k in zip(p_y, (1, 3, 2)):
+        cp.wait()
+        left_from(k)
+
     lc = rcopy(lts.at[pl.ds(NX * (1 - c), NX)], rcore, c_s.at[0], c_r.at[0], core_dev)
     lc.start()
     wait(w_x)
@@ -208,7 +217,11 @@
     s1[...] = lts[pl.ds(NX * c, NX)] + rcore[...]
     lx = [rcopy(s1.at[(x + k) % NX], rx.at[k], x_s.at[0, k], x_r.at[0, k], x_dev[k]) for k in range(1, NX)]
     start(lx)
+    wait(own_o)
+    grads_o(1)
+    contexts(1)
     wait(lx)
+    start(own_x[2:4])
     s2 = s1[x] + rx[1] + rx[2] + rx[3]
     for i in range(NZ - 1):
         sz[i] = s2[:, i * 128 : (i + 1) * 128]
@@ -224,27 +237,24 @@
         sy[k, 0:PR, :] = s3[k * PR : (k + 1) * PR, :]
     ly = [rcopy(sy.at[k], ry.at[k], y_s.at[0, k], y_r.at[0, k], y_dev[k]) for k in range(1, NY)]
     start(ly)
-    wait(own_o)
+    start(own_x[4:])
     start(fwd_o)
-    for slot in (1, 3):
-        grads_o(slot)
-        contexts(slot)
     wait(ly)
     gl[c, x, z] = sy[0] + ry[1] + ry[2] + ry[3]
     gz = [rcopy(gl.at[c, x, z], gl.at[c, x, z], z_s.at[1, k], z_r.at[1, k], z_dev[k]) for k in range(1, NZ)]
     start(gz)
+    grads_o(3)
+    wait(gz)
+    gx = [rcopy(gl.at[c, x], gl.at[c, x], x_s.at[1, k], x_r.at[1, k], x_dev[k]) for k in range(1, NX)]
+    start(gx)
+    contexts(3)
+    wait(gx)
+    gc = rcopy(gl.at[c], gl.at[c], c_s.at[1], c_r.at[1], core_dev)
+    gc.start()
     wait(own_x)
     start(fwd_x)
     q_y = [rcopy(cot.at[0:XC, token_cols(k)], qf.at[k], q_s.at[k], q_r.at[k], y_dev[NY - k]) for k in (1, 3, 2)]
     start(q_y)
-    wait(gz)
-    gx = [rcopy(gl.at[c, x], gl.at[c, x], x_s.at[1, k], x_r.at[1, k], x_dev[k]) for k in range(1, NX)]
-    start(gx)
-    grads_x(1)
-    wait(gx)
-    gc = rcopy(gl.at[c], gl.at[c], c_s.at[1], c_r.at[1], core_dev)
-    gc.start()
-    grads_x(3)
     gc.wait()
     for p in range(PIECES):
         for i in range(NZ - 1):
@@ -253,62 +263,105 @@
         left = lt[b * RANK : (b + 1) * RANK, :]
         bas[b * RANK : (b + 1) * RANK, :] = nn(inverse_factor(nt(left, left, PRECISE)), left, PRECISE)
 
+    grads_x(1)
+    grads_x(3)
+    qf[0] = cot[0:XC, token_cols(0)]
+    for i in range(2):
+        hi, mid, _ = split3(bas[i * RANK : (i + 2) * RANK, :])
+        terms = jnp.concatenate([hi, hi, mid, mid], axis=0).astype(F32)
+        bav[i] = terms.T.astype(BF16)
+    out_ba = pltpu.make_async_copy(bav, BA, st.at[3])
+    out_ba.start()
     wait(fwd_o)
     grads_o(2)
     contexts(2)
     out_gc = pltpu.make_async_copy(gcv, GC, st.at[1])
     out_gc.start()
+
+    rpart[...] = nt(bas[...], acc[...], PRECISE)
+    bas3 = jnp.concatenate(split3(bas[...]), axis=0)
     wait(fwd_x)
+    last = nt(bas3, xg[2])
+    last = jnp.concatenate(split3(last[:NR] + last[NR : 2 * NR] + last[2 * NR :]), axis=0)
+    last = nt(last, cot[0:XC, token_cols(2)])
+    rpart[:, 0:XC] += last[:NR] + last[NR : 2 * NR] + last[2 * NR :]
+    right = jnp.where(in_block((NR, PACK)), rpart[...] * scale, 0.0)
+    packed = right[:RANK] + right[RANK : 2 * RANK] + right[2 * RANK :]
+    hr = RANK // NC
+    for e in range(NC):
+        for i in range(NX):
+            q1[e, i] = packed[e * hr : (e + 1) * hr, i * 128 : (i + 1) * 128]
+    r1 = [rcopy(q1.at[(c + e) % NC, (x + k) % NX], rxr.at[e, k], r_s.at[0, e, k], r_r.at[0, e, k], row_dev[e, k])
+          for e, k in row]
+    start(r1)
     grads_x(2)
-    acc[...] = acc[...] * scale
-
-    right = jnp.where(in_block((NR, PACK)), nt(bas[...], acc[...], PRECISE), 0.0)
-    rt[...] = right[:RANK] + right[RANK : 2 * RANK] + right[2 * RANK :]
-    hr = RANK // NC
-    rc = rcopy(rt.at[pl.ds(pl.multiple_of((1 - c) * hr, 8), hr)], rcr, c_s.at[2], c_r.at[2], core_dev)
-    rc.start()
-    rc.wait()
-    s = rt[pl.ds(pl.multiple_of(c * hr, 8), hr), :] + rcr[...]
-    for i in range(NX):
-        q1[i] = s[:, i * 128 : (i + 1) * 128]
-    rxs = [rcopy(q1.at[(x + k) % NX], rxr.at[k], x_s.at[2, k], x_r.at[2, k], x_dev[k]) for k in range(1, NX)]
-    start(rxs)
-    wait(rxs)
-    q2[...] = q1[x] + rxr[1] + rxr[2] + rxr[3]
-    rzs = [rcopy(q2, rzr.at[k], z_s.at[2, k], z_r.at[2, k], z_dev[k]) for k in range(1, NZ)]
-    start(rzs)
-    nev[...] = acc[...].T - tn(bas[...], right, PRECISE)
+    wait(r1)
+    mine = q1[c, x]
+    for e, k in row:
+        mine = mine + rxr[e, k]
+    q2[...] = mine
+    r2 = [rcopy(q2, rzr.at[k], z_s.at[2, k], z_r.at[2, k], z_dev[k]) for k in range(1, NZ)]
+    start(r2)
+    nev[...] = acc[...].T * scale - tn(bas[...], right, PRECISE)
     out_ne = pltpu.make_async_copy(nev, NE, st.at[2])
     out_ne.start()
-    wait(rzs)
+    wait(r2)
     rzr[0] = q2[...]
     total = rzr[z % NZ]
     for i in range(1, NZ):
         total = total + rzr[(z + NZ - i) % NZ]
     gr[c, x] = total
-    rxg = [rcopy(gr.at[c, x], gr.at[c, x], x_s.at[3, k], x_r.at[3, k], x_dev[k]) for k in range(1, NX)]
-    start(rxg)
-    wait(rxg)
-    rcg = rcopy(gr.at[c], gr.at[c], c_s.at[3], c_r.at[3], core_dev)
-    rcg.start()
-    rcg.wait()
-    for p in range(NC):
-        for i in range(NX):
-            rtot[p * hr : (p + 1) * hr, i * 128 : (i + 1) * 128] = gr[p, i]
-    full = jnp.where(in_block((NR, PACK)), jnp.concatenate([rtot[...]] * NB, axis=0), 0.0)
-    cgv[...] = tn(bas[...], full, PRECISE)
-    out_cg = pltpu.make_async_copy(cgv, CG, st.at[3])
-    out_cg.start()
+    r3 = [rcopy(gr.at[c, x], gr.at[c, x], r_s.at[1, e, k], r_r.at[1, e, k], row_dev[e, k]) for e, k in row]
+    start(r3)
 
     w_c.wait()
     wait(q_y)
-    out = tn(cot[0:XC, token_cols(0)], wf[0, :, 0:D])
-    for k in range(1, NY):
-        out = out + tn(qf[k], wf[k, :, 0:D])
-    giv[...] = out.astype(BF16)
+    giv[...] = tn(qf[...].reshape(NY * XC, ROWS), wf[...].reshape(NY * XC, WL)[:, :D]).astype(BF16)
     out_gi = pltpu.make_async_copy(giv, GI, st.at[0])
     out_gi.start()
-    wait((out_gc, out_ne, out_cg, out_gi))
+    wait(r3)
+    out_gr = pltpu.make_async_copy(gr, GR, st.at[4])
+    out_gr.start()
+    wait((out_gc, out_ne, out_ba, out_gi, out_gr))
+
+
+def finish(GI, GC, NE, BA, GR, gi_out, gc_out, ne_out, cg_out, gi, gc, ne, ba, gr, cg, sem):
+    loads = [
+        pltpu.make_async_copy(a, b, sem.at[i])
+        for i, (a, b) in enumerate(((GR, gr), (BA, ba), (NE, ne), (GI, gi), (GC, gc)))
+    ]
+    for cp in loads:
+        cp.start()
+    loads[0].wait()
+    hr = RANK // NC
+    col = lax.broadcasted_iota(jnp.int32, (RANK, 256), 1)
+    rhs = []
+    for i, edge in ((0, QC), (1, XC - 256)):
+        total = jnp.concatenate(
+            [jnp.concatenate([gr[e, 2 * i], gr[e, 2 * i + 1]], axis=1) for e in range(NC)], axis=0
+        )
+        total = jnp.concatenate([jnp.where(col < edge, total, 0.0), jnp.where(col < edge, 0.0, total)], axis=0)
+        hi, mid, _ = split3(total)
+        rhs.append(jnp.concatenate([hi, mid, hi, mid], axis=0))
+    loads[1].wait()
+    stores = []
+
+    def store(src, dst):
+        cp = pltpu.make_async_copy(src, dst, sem.at[5 + len(stores)])
+        cp.start()
+        stores.append(cp)
+
+    half = D // 2
+    for r in range(2):
+        rows = pl.ds(r * half, half)
+        for i in range(2):
+            cg[rows, i * 256 : (i + 1) * 256] = nn(ba[i, rows, :], rhs[i])
+        store(cg.at[rows], cg_out.at[rows])
+    for cp, src, dst in zip(loads[2:], (ne, gi, gc), (ne_out, gi_out, gc_out)):
+        cp.wait()
+        store(src, dst)
+    for cp in stores:
+        cp.wait()
 
 
 def on_device(
@@ -327,26 +380,30 @@
         V((NX, NY * PR, D), F32), V((NZ, NY * PR, 128), F32), V((NZ, NY * PR, 128), F32),
         V((NY, 16, 128), F32), V((NY, 16, 128), F32), V((NC, NX, NZ, 16, 128), F32),
         V((NR, D), F32), V((NR, D), F32),
-        V((RANK, PACK), F32), V((hr, PACK), F32), V((NX, hr, 128), F32), V((NX, hr, 128), F32),
-        V((hr, 128), F32), V((NZ, hr, 128), F32), V((NC, NX, hr, 128), F32), V((RANK, PACK), F32),
-        V((ROWS, D), BF16), V((QC, TOK), BF16), V((D, PACK), F32), V((D, PACK), F32),
+        V((NR, PACK), F32), V((NC, NX, hr, 128), F32), V((NC, NX, hr, 128), F32),
+        V((hr, 128), F32), V((NZ, hr, 128), F32), V((NC, NX, hr, 128), F32),
+        V((ROWS, D), BF16), V((QC, TOK), BF16), V((D, PACK), F32), V((2, D, 256), BF16),
     ]
     S = pltpu.SemaphoreType.DMA
     sems = [
-        S((12,)), S((4,)), S((2, 4, 2)), S((2, 4, 2)), S((2, 2)), S((2, 2)), S((NY,)), S((NY,)),
+        S((12,)), S((5,)), S((2, 4, CH)), S((2, 4, CH)), S((2, CH)), S((2, CH)), S((NY,)), S((NY,)),
         S((5,)), S((5,)), S((4, NX)), S((4, NX)), S((3, NZ)), S((3, NZ)),
         S((NX,)), S((NX,)), S((2, NY)), S((2, NY)), S((NY,)), S((NY,)),
+        S((2, NC, NX)), S((2, NC, NX)),
     ]
-    grad_input, grad_context, new_error, compressed = pl.pallas_call(
+    outs = (
+        jax.ShapeDtypeStruct((ROWS, D), BF16),
+        jax.ShapeDtypeStruct((QC, TOK), BF16),
+        jax.ShapeDtypeStruct((D, PACK), F32),
+    )
+    parts = pl.pallas_call(
         body,
-        out_shape=(
-            jax.ShapeDtypeStruct((ROWS, D), BF16),
-            jax.ShapeDtypeStruct((QC, TOK), BF16),
-            jax.ShapeDtypeStruct((D, PACK), F32),
-            jax.ShapeDtypeStruct((D, PACK), F32),
+        out_shape=outs[:3] + (
+            jax.ShapeDtypeStruct((2, D, 256), BF16),
+            jax.ShapeDtypeStruct((NC, NX, hr, 128), F32),
         ),
         in_specs=[any_spec] * 12,
-        out_specs=(any_spec,) * 4,
+        out_specs=(any_spec,) * 5,
         scratch_shapes=scratch + sems,
         compiler_params=pltpu.CompilerParams(
             collective_id=0, has_side_effects=True, vmem_limit_bytes=60 * 2**20
@@ -356,6 +413,18 @@
         normed_input, grad_query.T, grad_key.T, grad_value.T, context.T, grad_output,
         w_query.T, w_key.T, w_value.T, w_output, error, factor_init.T,
     )
+    grad_input, grad_context, new_error, compressed = pl.pallas_call(
+        finish,
+        out_shape=outs + (jax.ShapeDtypeStruct((D, PACK), F32),),
+        in_specs=[any_spec] * 5,
+        out_specs=(any_spec,) * 4,
+        scratch_shapes=[
+            V((ROWS, D), BF16), V((QC, TOK), BF16), V((D, PACK), F32),
+            V((2, D, 256), BF16), V((NC, NX, hr, 128), F32), V((D, PACK), F32), S((10,)),
+        ],
+        compiler_params=pltpu.CompilerParams(vmem_limit_bytes=60 * 2**20),
+        name="finish",
+    )(*parts)
     return grad_input, grad_context.T, new_error, compressed
 
 

time: 120 us -> 107 us (0.89)
  Pallas kernels: 113 us -> 106 us
  local copies, waits for them, and re-layouts: 6.65 us -> 0 us
    pallas_call x1 -> x2, Pallas kernels: 113 us -> 106 us  [the longest x1 102 us: on_device(): pl.pallas_call(body, out_shape=outs[:3] + (jax.ShapeDtypeStruct((2, D, 25...]
    unnamed x10 -> x0, local copies, waits for them, and re-layouts: 6.65 us -> none
where the time goes in v2:
time: 107 us
  Pallas kernels  106 us (99%)
    pallas_call x1, Pallas kernels, on_device(): pl.pallas_call(body, out_shape=outs[:3] + (jax.ShapeDtypeStruct((2, D, 25...  102 us
    pallas_call x1, Pallas kernels, on_device(): pl.pallas_call(finish, out_shape=outs + (jax.ShapeDtypeStruct((D, PACK),...  4.02 us

profile of v2, /device:TPU:1, one launch (start us, length us, event | category | flops | bytes accessed | tf_op | source)
XLA Modules:
  0.0 106.5 jit_solution(5472905550381651119)
XLA Ops:
  0.6 101.7 %backward.1 = (bf16[512,896]{1,0:T(8,128)(2,1)}, bf16[224,2048]{1,0:T(8,128)(2,1)}, f32[896,512]{1,0:T(8,128)}, bf16[2,896,256]{2,1,0:T(8,128)(2,1)}, f32[2,4,16,128]{3,2,1,0:T(8,128)}) custom-call(bf16[512,896]{1,0:T(8,128)(2,1)} %X.1, bf16[224,2048]{1,0:T(8,128)(2,1)} %bitcast.9, bf16[32,2048]{1,0:T(8,128)(2,1)} %bitcast.12, bf16[32,2048]{1,0:T(8,128)(2,1)} %bitcast.13, ...), custom_call_target="tpu_custom_call" | custom-call | tf_op jit(solution)/shard_map/backward/pallas_call | solution.py:399
  102.4 4.0 %finish.1 = (bf16[512,896]{1,0:T(8,128)(2,1)}, bf16[224,2048]{1,0:T(8,128)(2,1)}, f32[896,512]{1,0:T(8,128)}, f32[896,512]{1,0:T(8,128)}) custom-call(bf16[512,896]{1,0:T(8,128)(2,1)} %get-tuple-element.13.GI, bf16[224,2048]{1,0:T(8,128)(2,1)} %get-tuple-element.14.GC, f32[896,512]{1,0:T(8,128)} %get-tuple-element.15.NE, ...), custom_call_target="tpu_custom_call" | custom-call | tf_op jit(solution)/shard_map/finish/pallas_call | solution.py:416

commit v3 on v2

--- a/solution.py
+++ b/solution.py
@@ -18,12 +18,15 @@
 PACK = 512
 XC = QC + 2 * KC
 WL = 1024
-WX = WL // 4
+WX = WL // NX
+SLOT = (0, 1, 3, 2)
 RANK = 32
 NB = 3
 NR = NB * RANK
 PIECES = NC * NX
-PR = NR // PIECES
+XR = 2 * RANK
+PR = XR // PIECES
+PO = RANK // PIECES
 WR = XC // NC
 
 
@@ -64,19 +67,20 @@
     )
 
 
-def inverse_factor(gram):
+def inverse_factors(grams):
     row = lax.broadcasted_iota(jnp.int32, (RANK, RANK), 0)
     col = lax.broadcasted_iota(jnp.int32, (RANK, RANK), 1)
     eye = (row == col).astype(F32)
-    work = jnp.concatenate([eye, gram], axis=1)
+    works = [jnp.concatenate([eye, gram], axis=1) for gram in grams]
     sub = lax.broadcasted_iota(jnp.int32, (RANK, 2 * RANK), 0)
     for k in range(RANK):
-        pivot = work[k : k + 1, RANK + k : RANK + k + 1]
-        inv = 1.0 / jnp.sqrt(pivot)
-        row_k = work[k : k + 1, :] * inv
-        col_k = work[:, RANK + k : RANK + k + 1] * inv
-        work = jnp.where(sub > k, work - col_k * row_k, jnp.where(sub == k, row_k, work))
-    return work[:, :RANK]
+        for b, work in enumerate(works):
+            pivot = work[k : k + 1, RANK + k : RANK + k + 1]
+            inv = 1.0 / jnp.sqrt(pivot)
+            row_k = work[k : k + 1, :] * inv
+            col_k = work[:, RANK + k : RANK + k + 1] * inv
+            works[b] = jnp.where(sub > k, work - col_k * row_k, jnp.where(sub == k, row_k, work))
+    return [work[:, :RANK] for work in works]
 
 
 def body(
@@ -84,8 +88,9 @@
     GI, GC, NE, BA, GR,
     xg, og, cot, wo, er, fi, wf, qf, acc,
     pts, ptr, lts, rcore, s1, rx, sz, rz, sy, ry, gl, lt, bas,
+    o1, orx, oz, orz, ol,
     rpart, q1, rxr, q2, rzr, gr,
-    giv, gcv, nev, bav,
+    gacc, giv, gcv, nev, bav,
     ld, st, ag_s, ag_r, fw_s, fw_r, p_s, p_r, c_s, c_r, x_s, x_r, z_s, z_r, w_s, w_r, y_s, y_r, q_s, q_r, r_s, r_r,
 ):
     d = lax.axis_index("dp")
@@ -111,7 +116,7 @@
             cp.wait()
 
     barrier = pltpu.get_barrier_semaphore()
-    peers = list(row_dev.values()) + z_dev[1:] + y_dev[1:]
+    peers = [z_dev[k] for k in (4, 3, 5, 2, 6, 1, 7)] + list(row_dev.values()) + y_dev[1:]
     for p in peers:
         pl.semaphore_signal(barrier, inc=1, device_id=p, device_id_type=MESH)
 
@@ -147,32 +152,35 @@
     start(own_o[:2])
 
     wrows, wcols = pl.ds(pl.multiple_of(c * WR, 16), WR), pl.ds(pl.multiple_of(x * WX, 128), WX)
-    w_y = [rcopy(wf.at[0, wrows, wcols], wf.at[k, wrows, wcols], y_s.at[1, k], y_r.at[1, k], y_dev[NY - k])
+    odd = z % 2
+    wtile = pl.ds(pl.multiple_of(x * WX + odd * (WX // 2), 128), WX // 2)
+    w_y = [rcopy(wf.at[0, wrows, wtile], wf.at[SLOT[k], wrows, wtile], y_s.at[1, k], y_r.at[1, k], y_dev[NY - k])
            for k in range(1, NY)]
     wait(loads[:3])
     start(w_y)
 
     wait(loads[3:8])
     fm = jnp.where(in_block((NR, PACK)), jnp.concatenate([fi[...]] * NB, axis=0), 0.0)
-    fm3 = jnp.concatenate(split3(fm), axis=0)
+    fm3 = jnp.concatenate(split3(fm[:XR, :XC]), axis=0)
 
     def token_cols(k):
         return pl.ds(pl.multiple_of(((y + NY - k) % NY) * ROWS, ROWS), ROWS)
 
     for k in (1, 3, 2, 0):
-        prod = nn(fm3, cot[:, token_cols(k)])
+        prod = nn(fm3, cot[0:XC, token_cols(k)])
         dst = ptr if k == 0 else pts
-        dst[k] = prod[:NR] + prod[NR : 2 * NR] + prod[2 * NR :]
+        dst[k] = prod[:XR] + prod[XR : 2 * XR] + prod[2 * XR :]
     p_y = [rcopy(pts.at[k], ptr.at[k], p_s.at[k], p_r.at[k], y_dev[NY - k]) for k in (1, 3, 2)]
     start(p_y)
 
     start(own_o[2:])
-    start(own_x[:2])
 
     wait(w_y)
+    w_z = rcopy(wf.at[pl.ds(1, NY - 1), wrows, wtile], wf.at[pl.ds(1, NY - 1), wrows, wtile],
+                w_s.at[0], w_r.at[0], dev(z + 1 - 2 * odd, x, c, y))
+    w_z.start()
     w_x = [rcopy(wf.at[pl.ds(1, NY - 1), wrows, wcols], wf.at[pl.ds(1, NY - 1), wrows, wcols],
                  w_s.at[k], w_r.at[k], x_dev[k]) for k in range(1, NX)]
-    start(w_x)
 
     def grads_x(slot):
         acc[0:XC, :] += nn(cot[0:XC, token_cols(slot)], xg[slot])
@@ -185,19 +193,17 @@
 
     scale = float(TOK) ** (-0.5)
     wait(loads[8:])
-    own_e = nt(fm, er[...], PRECISE)
+    own_e = nt(fm[:XR], er[...], PRECISE)
     acc[...] = er[...].T * (float(TOK) ** 0.5)
+    w_z.wait()
+    start(w_x)
     grads_x(0)
     grads_o(0)
     contexts(0)
 
     def left_from(k):
-        parts = split3(ptr[k])
-        up = nn(jnp.concatenate([t[: 2 * RANK] for t in parts], axis=0), xg[0])
-        lo = nn(jnp.concatenate([t[2 * RANK :] for t in parts], axis=0), og[0])
-        up = up[: 2 * RANK] + up[2 * RANK : 4 * RANK] + up[4 * RANK :]
-        lo = lo[:RANK] + lo[RANK : 2 * RANK] + lo[2 * RANK :]
-        left = jnp.concatenate([up, lo], axis=0) * scale
+        left = nn(jnp.concatenate(split3(ptr[k]), axis=0), xg[0])
+        left = (left[:XR] + left[XR : 2 * XR] + left[2 * XR :]) * scale
         if k == 0:
             left = left + own_e
         for p in range(PIECES):
@@ -207,6 +213,9 @@
     for cp, k in zip(p_y, (1, 3, 2)):
         cp.wait()
         left_from(k)
+
+    wait(own_o[:2])
+    start(fwd_o[:2])
 
     lc = rcopy(lts.at[pl.ds(NX * (1 - c), NX)], rcore, c_s.at[0], c_r.at[0], core_dev)
     lc.start()
@@ -217,11 +226,11 @@
     s1[...] = lts[pl.ds(NX * c, NX)] + rcore[...]
     lx = [rcopy(s1.at[(x + k) % NX], rx.at[k], x_s.at[0, k], x_r.at[0, k], x_dev[k]) for k in range(1, NX)]
     start(lx)
-    wait(own_o)
+    wait(own_o[2:])
+    start(fwd_o[2:])
+    start(own_x[:2])
     grads_o(1)
-    contexts(1)
     wait(lx)
-    start(own_x[2:4])
     s2 = s1[x] + rx[1] + rx[2] + rx[3]
     for i in range(NZ - 1):
         sz[i] = s2[:, i * 128 : (i + 1) * 128]
@@ -232,36 +241,74 @@
     s3 = sz[z]
     for k in range(1, NZ):
         s3 = s3 + rz[k]
-    sy[...] = jnp.zeros_like(sy)
     for k in range(NY):
-        sy[k, 0:PR, :] = s3[k * PR : (k + 1) * PR, :]
+        sy[k] = s3[k * PR : (k + 1) * PR, :]
     ly = [rcopy(sy.at[k], ry.at[k], y_s.at[0, k], y_r.at[0, k], y_dev[k]) for k in range(1, NY)]
     start(ly)
-    start(own_x[4:])
-    start(fwd_o)
+    start(own_x[2:])
+    grads_o(3)
+    contexts(1)
+
+    wait(fwd_o)
+    grads_o(2)
+    left_o = nn(fm[XR:], acc[...], PRECISE) * scale
+    for p in range(PIECES):
+        o1[p // NX, p % NX, 0:PO, :] = left_o[p * PO : (p + 1) * PO, :]
+        o1[p // NX, p % NX, PO:, :] = jnp.zeros((8 - PO, D), F32)
+    oa = [rcopy(o1.at[(c + e) % NC, (x + k) % NX], orx.at[e, k], r_s.at[2, e, k], r_r.at[2, e, k], row_dev[e, k])
+          for e, k in row]
+    start(oa)
+    contexts(3)
     wait(ly)
     gl[c, x, z] = sy[0] + ry[1] + ry[2] + ry[3]
     gz = [rcopy(gl.at[c, x, z], gl.at[c, x, z], z_s.at[1, k], z_r.at[1, k], z_dev[k]) for k in range(1, NZ)]
     start(gz)
-    grads_o(3)
+    wait(oa)
+    o2 = o1[c, x]
+    for e, k in row:
+        o2 = o2 + orx[e, k]
+    for i in range(NZ - 1):
+        oz[i] = o2[:, i * 128 : (i + 1) * 128]
+    oz[NZ - 1] = jnp.zeros_like(oz[NZ - 1])
+    ob = [rcopy(oz.at[(z + k) % NZ], orz.at[k], z_s.at[3, k], z_r.at[3, k], z_dev[k]) for k in range(1, NZ)]
+    start(ob)
+    contexts(2)
+    out_gc = pltpu.make_async_copy(gcv, GC, st.at[1])
+    out_gc.start()
     wait(gz)
     gx = [rcopy(gl.at[c, x], gl.at[c, x], x_s.at[1, k], x_r.at[1, k], x_dev[k]) for k in range(1, NX)]
     start(gx)
-    contexts(3)
+    wait(ob)
+    o3 = oz[z]
+    for k in range(1, NZ):
+        o3 = o3 + orz[k]
+    ol[c, x, z] = o3
+    oc = [rcopy(ol.at[c, x, z], ol.at[c, x, z], z_s.at[4, k], z_r.at[4, k], z_dev[k]) for k in range(1, NZ)]
+    start(oc)
     wait(gx)
     gc = rcopy(gl.at[c], gl.at[c], c_s.at[1], c_r.at[1], core_dev)
     gc.start()
-    wait(own_x)
-    start(fwd_x)
-    q_y = [rcopy(cot.at[0:XC, token_cols(k)], qf.at[k], q_s.at[k], q_r.at[k], y_dev[NY - k]) for k in (1, 3, 2)]
-    start(q_y)
+    wait(oc)
+    od = [rcopy(ol.at[c, x], ol.at[c, x], r_s.at[3, e, k], r_r.at[3, e, k], row_dev[e, k]) for e, k in row]
+    start(od)
+    wait(own_x[:2])
+    start(fwd_x[:2])
     gc.wait()
     for p in range(PIECES):
         for i in range(NZ - 1):
-            lt[p * PR : (p + 1) * PR, i * 128 : (i + 1) * 128] = gl[p // NX, p % NX, i, 0:PR, :]
+            lt[p * PR : (p + 1) * PR, i * 128 : (i + 1) * 128] = gl[p // NX, p % NX, i]
+    wait(od)
+    for p in range(PIECES):
+        for i in range(NZ - 1):
+            lt[XR + p * PO : XR + (p + 1) * PO, i * 128 : (i + 1) * 128] = ol[p // NX, p % NX, i, 0:PO, :]
+    wait(own_x[2:])
+    start(fwd_x[2:])
+    q_y = [rcopy(cot.at[0:XC, token_cols(k)], qf.at[SLOT[k]], q_s.at[k], q_r.at[k], y_dev[NY - k]) for k in (1, 3, 2)]
+    start(q_y)
+    lefts = [lt[b * RANK : (b + 1) * RANK, :] for b in range(NB)]
+    inverses = inverse_factors([nt(left, left, PRECISE) for left in lefts])
     for b in range(NB):
-        left = lt[b * RANK : (b + 1) * RANK, :]
-        bas[b * RANK : (b + 1) * RANK, :] = nn(inverse_factor(nt(left, left, PRECISE)), left, PRECISE)
+        bas[b * RANK : (b + 1) * RANK, :] = nn(inverses[b], lefts[b], PRECISE)
 
     grads_x(1)
     grads_x(3)
@@ -272,19 +319,22 @@
         bav[i] = terms.T.astype(BF16)
     out_ba = pltpu.make_async_copy(bav, BA, st.at[3])
     out_ba.start()
-    wait(fwd_o)
-    grads_o(2)
-    contexts(2)
-    out_gc = pltpu.make_async_copy(gcv, GC, st.at[1])
-    out_gc.start()
 
     rpart[...] = nt(bas[...], acc[...], PRECISE)
     bas3 = jnp.concatenate(split3(bas[...]), axis=0)
-    wait(fwd_x)
-    last = nt(bas3, xg[2])
-    last = jnp.concatenate(split3(last[:NR] + last[NR : 2 * NR] + last[2 * NR :]), axis=0)
-    last = nt(last, cot[0:XC, token_cols(2)])
-    rpart[:, 0:XC] += last[:NR] + last[NR : 2 * NR] + last[2 * NR :]
+
+    def last_rows(first, size):
+        part = nt(bas3, xg[2, first : first + size, :])
+        part = jnp.concatenate(split3(part[:NR] + part[NR : 2 * NR] + part[2 * NR :]), axis=0)
+        begin = ((y + NY - 2) % NY) * ROWS + first
+        part = nt(part, cot[0:XC, pl.ds(pl.multiple_of(begin, 128), size)])
+        rpart[:, 0:XC] += part[:NR] + part[NR : 2 * NR] + part[2 * NR :]
+
+    wait(fwd_x[:2])
+    last_rows(0, CHR)
+    last_rows(3 * CHR, CHR)
+    wait(fwd_x[2:])
+    last_rows(CHR, 2 * CHR)
     right = jnp.where(in_block((NR, PACK)), rpart[...] * scale, 0.0)
     packed = right[:RANK] + right[RANK : 2 * RANK] + right[2 * RANK :]
     hr = RANK // NC
@@ -315,13 +365,16 @@
     start(r3)
 
     w_c.wait()
-    wait(q_y)
-    giv[...] = tn(qf[...].reshape(NY * XC, ROWS), wf[...].reshape(NY * XC, WL)[:, :D]).astype(BF16)
-    out_gi = pltpu.make_async_copy(giv, GI, st.at[0])
-    out_gi.start()
+    wait(q_y[:2])
+    near = NY - 1
+    gacc[...] = tn(qf[0:near].reshape(near * XC, ROWS), wf[0:near].reshape(near * XC, WL)[:, :D])
     wait(r3)
     out_gr = pltpu.make_async_copy(gr, GR, st.at[4])
     out_gr.start()
+    q_y[2].wait()
+    giv[...] = (gacc[...] + tn(qf[near], wf[near, :, 0:D])).astype(BF16)
+    out_gi = pltpu.make_async_copy(giv, GI, st.at[0])
+    out_gi.start()
     wait((out_gc, out_ne, out_ba, out_gi, out_gr))
 
 
@@ -375,21 +428,23 @@
         V((NY, ROWS, D), BF16), V((NY, ROWS, D), BF16), V((PACK, TOK), BF16),
         V((QC, D), BF16), V((D, PACK), F32), V((RANK, PACK), F32),
         V((NY, XC, WL), BF16), V((NY, XC, ROWS), BF16), V((PACK, D), F32),
-        V((NY, NR, ROWS), F32), V((NY, NR, ROWS), F32),
+        V((NY, XR, ROWS), F32), V((NY, XR, ROWS), F32),
         V((PIECES, NY * PR, D), F32), V((NX, NY * PR, D), F32), V((NX, NY * PR, D), F32),
         V((NX, NY * PR, D), F32), V((NZ, NY * PR, 128), F32), V((NZ, NY * PR, 128), F32),
-        V((NY, 16, 128), F32), V((NY, 16, 128), F32), V((NC, NX, NZ, 16, 128), F32),
+        V((NY, PR, 128), F32), V((NY, PR, 128), F32), V((NC, NX, NZ, PR, 128), F32),
         V((NR, D), F32), V((NR, D), F32),
+        V((NC, NX, 8, D), F32), V((NC, NX, 8, D), F32), V((NZ, 8, 128), F32), V((NZ, 8, 128), F32),
+        V((NC, NX, NZ, 8, 128), F32),
         V((NR, PACK), F32), V((NC, NX, hr, 128), F32), V((NC, NX, hr, 128), F32),
         V((hr, 128), F32), V((NZ, hr, 128), F32), V((NC, NX, hr, 128), F32),
-        V((ROWS, D), BF16), V((QC, TOK), BF16), V((D, PACK), F32), V((2, D, 256), BF16),
+        V((ROWS, D), F32), V((ROWS, D), BF16), V((QC, TOK), BF16), V((D, PACK), F32), V((2, D, 256), BF16),
     ]
     S = pltpu.SemaphoreType.DMA
     sems = [
         S((12,)), S((5,)), S((2, 4, CH)), S((2, 4, CH)), S((2, CH)), S((2, CH)), S((NY,)), S((NY,)),
-        S((5,)), S((5,)), S((4, NX)), S((4, NX)), S((3, NZ)), S((3, NZ)),
+        S((5,)), S((5,)), S((4, NX)), S((4, NX)), S((5, NZ)), S((5, NZ)),
         S((NX,)), S((NX,)), S((2, NY)), S((2, NY)), S((NY,)), S((NY,)),
-        S((2, NC, NX)), S((2, NC, NX)),
+        S((4, NC, NX)), S((4, NC, NX)),
     ]
     outs = (
         jax.ShapeDtypeStruct((ROWS, D), BF16),

time: 107 us -> 103 us (0.963)
  Pallas kernels: 106 us -> 102 us
    pallas_call x1, Pallas kernels: 102 us -> 98.3 us  [on_device(): pl.pallas_call(body, out_shape=outs[:3] + (jax.ShapeDtypeStruct((2, D, 25...]
where the time goes in v3:
time: 103 us
  Pallas kernels  102 us (99%)
    pallas_call x1, Pallas kernels, on_device(): pl.pallas_call(body, out_shape=outs[:3] + (jax.ShapeDtypeStruct((2, D, 25...  98.3 us
    pallas_call x1, Pallas kernels, on_device(): pl.pallas_call(finish, out_shape=outs + (jax.ShapeDtypeStruct((D, PACK),...  4.02 us

profile of v3, /device:TPU:1, one launch (start us, length us, event | category | flops | bytes accessed | tf_op | source)
XLA Modules:
  0.0 103.1 jit_solution(3020577222947692284)
XLA Ops:
  0.6 98.3 %backward.1 = (bf16[512,896]{1,0:T(8,128)(2,1)}, bf16[224,2048]{1,0:T(8,128)(2,1)}, f32[896,512]{1,0:T(8,128)}, bf16[2,896,256]{2,1,0:T(8,128)(2,1)}, f32[2,4,16,128]{3,2,1,0:T(8,128)}) custom-call(bf16[512,896]{1,0:T(8,128)(2,1)} %X.1, bf16[224,2048]{1,0:T(8,128)(2,1)} %bitcast.9, bf16[32,2048]{1,0:T(8,128)(2,1)} %bitcast.12, bf16[32,2048]{1,0:T(8,128)(2,1)} %bitcast.13, ...), custom_call_target="tpu_custom_call" | custom-call | tf_op jit(solution)/shard_map/backward/pallas_call | solution.py:454
  98.9 4.0 %finish.1 = (bf16[512,896]{1,0:T(8,128)(2,1)}, bf16[224,2048]{1,0:T(8,128)(2,1)}, f32[896,512]{1,0:T(8,128)}, f32[896,512]{1,0:T(8,128)}) custom-call(bf16[512,896]{1,0:T(8,128)(2,1)} %get-tuple-element.13.GI, bf16[224,2048]{1,0:T(8,128)(2,1)} %get-tuple-element.14.GC, f32[896,512]{1,0:T(8,128)} %get-tuple-element.15.NE, ...), custom_call_target="tpu_custom_call" | custom-call | tf_op jit(solution)/shard_map/finish/pallas_call | solution.py:471

commit v4 on v3

--- a/solution.py
+++ b/solution.py
@@ -104,7 +104,7 @@
     x_dev = [dev(z, (x + k) % NX, c, y) for k in range(NX)]
     z_dev = [dev((z + k) % NZ, x, c, y) for k in range(NZ)]
     y_dev = [dev(z, x, c, (y + k) % NY) for k in range(NY)]
-    row = [(e, k) for k in range(NX) for e in range(NC)][1:]
+    row = [(e, k) for k in (2, 1, 3, 0) for e in range(NC) if e + k > 0]
     row_dev = {(e, k): dev(z, (x + k) % NX, (c + e) % NC, y) for e, k in row}
 
     def start(copies):
@@ -272,6 +272,8 @@
     oz[NZ - 1] = jnp.zeros_like(oz[NZ - 1])
     ob = [rcopy(oz.at[(z + k) % NZ], orz.at[k], z_s.at[3, k], z_r.at[3, k], z_dev[k]) for k in range(1, NZ)]
     start(ob)
+    wait(own_x[:2])
+    start(fwd_x[:2])
     contexts(2)
     out_gc = pltpu.make_async_copy(gcv, GC, st.at[1])
     out_gc.start()
@@ -291,8 +293,10 @@
     wait(oc)
     od = [rcopy(ol.at[c, x], ol.at[c, x], r_s.at[3, e, k], r_r.at[3, e, k], row_dev[e, k]) for e, k in row]
     start(od)
-    wait(own_x[:2])
-    start(fwd_x[:2])
+    wait(own_x[2:])
+    start(fwd_x[2:])
+    q_y = [rcopy(cot.at[0:XC, token_cols(k)], qf.at[SLOT[k]], q_s.at[k], q_r.at[k], y_dev[NY - k]) for k in (1, 3, 2)]
+    start(q_y)
     gc.wait()
     for p in range(PIECES):
         for i in range(NZ - 1):
@@ -301,10 +305,6 @@
     for p in range(PIECES):
         for i in range(NZ - 1):
             lt[XR + p * PO : XR + (p + 1) * PO, i * 128 : (i + 1) * 128] = ol[p // NX, p % NX, i, 0:PO, :]
-    wait(own_x[2:])
-    start(fwd_x[2:])
-    q_y = [rcopy(cot.at[0:XC, token_cols(k)], qf.at[SLOT[k]], q_s.at[k], q_r.at[k], y_dev[NY - k]) for k in (1, 3, 2)]
-    start(q_y)
     lefts = [lt[b * RANK : (b + 1) * RANK, :] for b in range(NB)]
     inverses = inverse_factors([nt(left, left, PRECISE) for left in lefts])
     for b in range(NB):
@@ -350,7 +350,7 @@
     for e, k in row:
         mine = mine + rxr[e, k]
     q2[...] = mine
-    r2 = [rcopy(q2, rzr.at[k], z_s.at[2, k], z_r.at[2, k], z_dev[k]) for k in range(1, NZ)]
+    r2 = [rcopy(q2, rzr.at[k], z_s.at[2, k], z_r.at[2, k], z_dev[k]) for k in (4, 3, 5, 2, 6, 1, 7)]
     start(r2)
     nev[...] = acc[...].T * scale - tn(bas[...], right, PRECISE)
     out_ne = pltpu.make_async_copy(nev, NE, st.at[2])
@@ -361,20 +361,20 @@
     for i in range(1, NZ):
         total = total + rzr[(z + NZ - i) % NZ]
     gr[c, x] = total
-    r3 = [rcopy(gr.at[c, x], gr.at[c, x], r_s.at[1, e, k], r_r.at[1, e, k], row_dev[e, k]) for e, k in row]
+    r3 = [rcopy(gr.at[c, x], GR.at[c, x], r_s.at[1, e, k], r_r.at[1, e, k], row_dev[e, k]) for e, k in row]
     start(r3)
+    out_gr = pltpu.make_async_copy(gr.at[c, x], GR.at[c, x], st.at[4])
+    out_gr.start()
 
     w_c.wait()
     wait(q_y[:2])
     near = NY - 1
     gacc[...] = tn(qf[0:near].reshape(near * XC, ROWS), wf[0:near].reshape(near * XC, WL)[:, :D])
-    wait(r3)
-    out_gr = pltpu.make_async_copy(gr, GR, st.at[4])
-    out_gr.start()
     q_y[2].wait()
     giv[...] = (gacc[...] + tn(qf[near], wf[near, :, 0:D])).astype(BF16)
     out_gi = pltpu.make_async_copy(giv, GI, st.at[0])
     out_gi.start()
+    wait(r3)
     wait((out_gc, out_ne, out_ba, out_gi, out_gr))
 
 

time: 103 us -> 101 us (0.981)
  Pallas kernels: 102 us -> 100 us
    pallas_call x1, Pallas kernels: 98.3 us -> 96.2 us  [on_device(): pl.pallas_call(body, out_shape=outs[:3] + (jax.ShapeDtypeStruct((2, D, 25...]
where the time goes in v4:
time: 101 us
  Pallas kernels  100 us (99%)
    pallas_call x1, Pallas kernels, on_device(): pl.pallas_call(body, out_shape=outs[:3] + (jax.ShapeDtypeStruct((2, D, 25...  96.2 us
    pallas_call x1, Pallas kernels, on_device(): pl.pallas_call(finish, out_shape=outs + (jax.ShapeDtypeStruct((D, PACK),...  4.02 us

profile of v4, /device:TPU:1, one launch (start us, length us, event | category | flops | bytes accessed | tf_op | source)
XLA Modules:
  0.0 101.0 jit_solution(3415406033242936516)
XLA Ops:
  0.6 96.2 %backward.1 = (bf16[512,896]{1,0:T(8,128)(2,1)}, bf16[224,2048]{1,0:T(8,128)(2,1)}, f32[896,512]{1,0:T(8,128)}, bf16[2,896,256]{2,1,0:T(8,128)(2,1)}, f32[2,4,16,128]{3,2,1,0:T(8,128)}) custom-call(bf16[512,896]{1,0:T(8,128)(2,1)} %X.1, bf16[224,2048]{1,0:T(8,128)(2,1)} %bitcast.9, bf16[32,2048]{1,0:T(8,128)(2,1)} %bitcast.12, bf16[32,2048]{1,0:T(8,128)(2,1)} %bitcast.13, ...), custom_call_target="tpu_custom_call" | custom-call | tf_op jit(solution)/shard_map/backward/pallas_call | solution.py:454
  96.8 4.0 %finish.1 = (bf16[512,896]{1,0:T(8,128)(2,1)}, bf16[224,2048]{1,0:T(8,128)(2,1)}, f32[896,512]{1,0:T(8,128)}, f32[896,512]{1,0:T(8,128)}) custom-call(bf16[512,896]{1,0:T(8,128)(2,1)} %get-tuple-element.13.GI, bf16[224,2048]{1,0:T(8,128)(2,1)} %get-tuple-element.14.GC, f32[896,512]{1,0:T(8,128)} %get-tuple-element.15.NE, ...), custom_call_target="tpu_custom_call" | custom-call | tf_op jit(solution)/shard_map/finish/pallas_call | solution.py:471

commit v5 on v4

--- a/solution.py
+++ b/solution.py
@@ -321,14 +321,14 @@
     out_ba.start()
 
     rpart[...] = nt(bas[...], acc[...], PRECISE)
-    bas3 = jnp.concatenate(split3(bas[...]), axis=0)
+    bas2 = jnp.concatenate(split3(bas[...])[:2], axis=0)
 
     def last_rows(first, size):
-        part = nt(bas3, xg[2, first : first + size, :])
-        part = jnp.concatenate(split3(part[:NR] + part[NR : 2 * NR] + part[2 * NR :]), axis=0)
+        part = nt(bas2, xg[2, first : first + size, :])
+        part = jnp.concatenate(split3(part[:NR] + part[NR:])[:2], axis=0)
         begin = ((y + NY - 2) % NY) * ROWS + first
         part = nt(part, cot[0:XC, pl.ds(pl.multiple_of(begin, 128), size)])
-        rpart[:, 0:XC] += part[:NR] + part[NR : 2 * NR] + part[2 * NR :]
+        rpart[:, 0:XC] += part[:NR] + part[NR:]
 
     wait(fwd_x[:2])
     last_rows(0, CHR)

time: 101 us -> 101 us (level)
  no operation moved by 1% of the time
where the time goes in v5:
time: 101 us
  Pallas kernels  100 us (99%)
    pallas_call x1, Pallas kernels, on_device(): pl.pallas_call(body, out_shape=outs[:3] + (jax.ShapeDtypeStruct((2, D, 25...  96.1 us
    pallas_call x1, Pallas kernels, on_device(): pl.pallas_call(finish, out_shape=outs + (jax.ShapeDtypeStruct((D, PACK),...  4.02 us

profile of v5, /device:TPU:1, one launch (start us, length us, event | category | flops | bytes accessed | tf_op | source)
XLA Modules:
  0.0 101.0 jit_solution(5513672524599808886)
XLA Ops:
  0.6 96.1 %backward.1 = (bf16[512,896]{1,0:T(8,128)(2,1)}, bf16[224,2048]{1,0:T(8,128)(2,1)}, f32[896,512]{1,0:T(8,128)}, bf16[2,896,256]{2,1,0:T(8,128)(2,1)}, f32[2,4,16,128]{3,2,1,0:T(8,128)}) custom-call(bf16[512,896]{1,0:T(8,128)(2,1)} %X.1, bf16[224,2048]{1,0:T(8,128)(2,1)} %bitcast.9, bf16[32,2048]{1,0:T(8,128)(2,1)} %bitcast.12, bf16[32,2048]{1,0:T(8,128)(2,1)} %bitcast.13, ...), custom_call_target="tpu_custom_call" | custom-call | tf_op jit(solution)/shard_map/backward/pallas_call | solution.py:454
  96.8 4.0 %finish.1 = (bf16[512,896]{1,0:T(8,128)(2,1)}, bf16[224,2048]{1,0:T(8,128)(2,1)}, f32[896,512]{1,0:T(8,128)}, f32[896,512]{1,0:T(8,128)}) custom-call(bf16[512,896]{1,0:T(8,128)(2,1)} %get-tuple-element.13.GI, bf16[224,2048]{1,0:T(8,128)(2,1)} %get-tuple-element.14.GC, f32[896,512]{1,0:T(8,128)} %get-tuple-element.15.NE, ...), custom_call_target="tpu_custom_call" | custom-call | tf_op jit(solution)/shard_map/finish/pallas_call | solution.py:471
